TPU v7x, 32 devices: a whole 2x2x4 slice. The times are simulated.
32 devices in a mesh: seq: 4 (over x, core), ctx: 8 (over z, y).
Axes of the slice: x: 2, y: 2, z: 4, core: 2. Of those that a mesh axis runs over, the one named last changes fastest.
Arguments:
- tokens: bfloat16 [3, 4, 768, 767], P(None, 'seq', 'ctx'), may hold values from -6 to 6
- segment_ids: int32 [3, 4, 768], P(None, 'seq'), may hold values from 0 to 7, never falling along the last dimension, each value on 1 to 576 neighbouring positions
- qkv_weight: bfloat16 [768, 2304], P(('seq', 'ctx')), may hold values from -0.21875 to 0.21875
- out_weight: bfloat16 [768, 767], P(('seq', 'ctx')), may hold values from -0.875 to 0.875
- up_weight: bfloat16 [768, 3072], P(('seq', 'ctx')), may hold values from -0.21875 to 0.21875
- down_weight: bfloat16 [3072, 767], P(('seq', 'ctx')), may hold values from -0.109375 to 0.109375
- attn_gain: bfloat16 [768], P(('seq', 'ctx')), may hold values from 0.099609375 to 1.8984375
- mlp_gain: bfloat16 [768], P(('seq', 'ctx')), may hold values from 0.099609375 to 1.8984375
- out_cotangent: bfloat16 [3, 4, 768, 767], P(None, 'seq', 'ctx'), may hold values from -6 to 6
Outputs:
- result: float32 [3, 4, 768, 767], P(None, 'seq', 'ctx')
- grad_tokens: float32 [3, 4, 768, 767], P(None, 'seq', 'ctx')
- grad_qkv_weight: float32 [768, 2304], P(('seq', 'ctx'))
- grad_out_weight: float32 [768, 767], P(('seq', 'ctx'))
- grad_up_weight: float32 [768, 3072], P(('seq', 'ctx'))
- grad_down_weight: float32 [3072, 767], P(('seq', 'ctx'))
- grad_attn_gain: float32 [768], P(('seq', 'ctx'))
- grad_mlp_gain: float32 [768], P(('seq', 'ctx'))
Inputs may be any that keep to these rules, and one draw needn't show every extreme that they name: `segment_ids`: along each sequence the ids never fall; each of the 8 documents of a sequence has 1 to 576 tokens, and one has exactly 576.
All inputs are finite; a program needn't handle non-finite values.
Results may differ from a plain program's by a relative error of at most 0.014.
Values may be sent and summed in bfloat16 or wider, within the bound.
No kernel may reach another device: no remote copies, remote signals or barrier semaphores. Data moves between devices by JAX's collectives and lax.ppermute only.
A program may use at most 384 MiB of HBM per device.

v0:
```python
import math
import jax
import jax.numpy as jnp
from jax import lax
from jax.sharding import PartitionSpec as P

HEADS = 12
HEAD_DIM = 64
EPS = 1e-05
NEG = -1e30
SCALE = 0.125


def crms(inputs, gains):
    totals = jnp.sum(inputs, axis=-1, keepdims=True)
    meansq = (jnp.sum(inputs * inputs, axis=-1, keepdims=True) + totals * totals) / gains.shape[0]
    return jnp.concatenate([inputs, -totals], axis=-1) * lax.rsqrt(meansq + EPS) * gains


def gelu_tanh(inputs):
    return jax.nn.gelu(inputs, approximate=True)


def matmul(left, right):
    return jnp.dot(left, right, preferred_element_type=jnp.float32)


def matmul_left_t(left, right):
    return lax.dot_general(
        left, right, (((0,), (0,)), ((), ())), preferred_element_type=jnp.float32
    )


def matmul_right_t(left, right):
    return lax.dot_general(
        left, right, (((1,), (1,)), ((), ())), preferred_element_type=jnp.float32
    )


def allowed_pairs(query_pos, query_seg, key_pos, key_seg):
    same_doc = query_seg[:, None, :, None] == key_seg[:, None, None, :]
    causal = query_pos[None, None, :, None] >= key_pos[None, None, None, :]
    return same_doc & causal


def attend_block(state, queries, query_pos, query_seg, keys, values, key_pos, key_seg):
    best, denom, accum = state
    scores = (
        jnp.einsum("bqhd,bkhd->bhqk", queries, keys, preferred_element_type=jnp.float32) * SCALE
    )
    allowed = allowed_pairs(query_pos, query_seg, key_pos, key_seg)
    scores = jnp.where(allowed, scores, NEG)
    peak = jnp.maximum(best, jnp.max(scores, axis=-1))
    weights = jnp.where(allowed, jnp.exp(scores - peak[..., None]), 0.0)
    factor = jnp.exp(best - peak)
    denom = denom * factor + jnp.sum(weights, axis=-1)
    accum = accum * factor[..., None] + jnp.einsum(
        "bhqk,bkhd->bhqd", weights.astype(jnp.bfloat16), values, preferred_element_type=jnp.float32
    )
    return (peak, denom, accum)


def pair_grads(queries, grad_o, lse, delta, query_pos, query_seg, keys, values, key_pos, key_seg):
    scores = (
        jnp.einsum("bqhd,bkhd->bhqk", queries, keys, preferred_element_type=jnp.float32) * SCALE
    )
    allowed = allowed_pairs(query_pos, query_seg, key_pos, key_seg)
    probs = jnp.where(allowed, jnp.exp(scores - lse[..., None]), 0.0)
    dprobs = jnp.einsum("bqhd,bkhd->bhqk", grad_o, values, preferred_element_type=jnp.float32)
    grad_scores = (probs * (dprobs - delta[..., None])).astype(jnp.bfloat16)
    part_q = (
        jnp.einsum("bhqk,bkhd->bqhd", grad_scores, keys, preferred_element_type=jnp.float32) * SCALE
    )
    part_k = (
        jnp.einsum("bhqk,bqhd->bkhd", grad_scores, queries, preferred_element_type=jnp.float32)
        * SCALE
    )
    part_v = jnp.einsum(
        "bhqk,bqhd->bkhd", probs.astype(jnp.bfloat16), grad_o, preferred_element_type=jnp.float32
    )
    return (part_q, part_k, part_v)


def body(
    tokens,
    segment_ids,
    qkv_weight,
    out_weight,
    up_weight,
    down_weight,
    attn_gain,
    mlp_gain,
    out_cotangent,
):
    micro_count, seq_count, local_len, res_width = tokens.shape
    length = segment_ids.shape[2]
    first = lax.axis_index("ctx") * local_len
    query_pos = first + jnp.arange(local_len, dtype=jnp.int32)
    row_count = seq_count * local_len

    def fetch():
        return (
            lax.all_gather(qkv_weight, ("seq", "ctx"), axis=0, tiled=True),
            lax.all_gather(out_weight, ("seq", "ctx"), axis=0, tiled=True),
            lax.all_gather(up_weight, ("seq", "ctx"), axis=0, tiled=True),
            lax.all_gather(down_weight, ("seq", "ctx"), axis=0, tiled=True),
            lax.all_gather(attn_gain, ("seq", "ctx"), axis=0, tiled=True),
            lax.all_gather(mlp_gain, ("seq", "ctx"), axis=0, tiled=True),
        )

    def backward(number, gathered, saved):
        qkv_full, out_full, up_full, down_full, gain_one, gain_two = gathered
        (
            inputs,
            seg_rows,
            query_seg,
            norm_a,
            queries,
            keys_own,
            values_own,
            attn_f32,
            lse,
            attn,
            mixed,
            norm_m,
            pre,
            act,
        ) = saved
        width = qkv_full.shape[0]
        grad_y = out_cotangent[number].reshape(row_count, res_width)
        grad_down = matmul_left_t(act, grad_y)
        grad_act = matmul_right_t(grad_y, down_full)
        _, gelu_pull = jax.vjp(gelu_tanh, pre)
        grad_pre = gelu_pull(grad_act)[0].astype(jnp.bfloat16)
        grad_up = matmul_left_t(norm_m, grad_pre)
        grad_norm_m = matmul_right_t(grad_pre, up_full)
        _, pull_two = jax.vjp(crms, mixed, gain_two.astype(jnp.float32))
        grad_mixed_norm, grad_gain_two = pull_two(grad_norm_m)
        grad_mixed = grad_y.astype(jnp.float32) + grad_mixed_norm
        grad_branch = grad_mixed.astype(jnp.bfloat16)
        grad_outw = matmul_left_t(attn, grad_branch)
        grad_attn = (
            matmul_right_t(grad_branch, out_full)
            .astype(jnp.bfloat16)
            .reshape(seq_count, local_len, HEADS, HEAD_DIM)
        )
        delta = jnp.transpose(jnp.sum(grad_attn.astype(jnp.float32) * attn_f32, axis=-1), (0, 2, 1))
        block_len = math.gcd(length, 1024)
        block_ids = jnp.arange(length // block_len, dtype=jnp.int32)
        keys_all, values_all = (
            lax.all_gather(keys_own, "ctx", axis=1, tiled=True),
            lax.all_gather(values_own, "ctx", axis=1, tiled=True),
        )

        def back_keys(carry, number_block):
            offset = number_block * block_len
            key_block = lax.dynamic_slice_in_dim(keys_all, offset, block_len, 1)
            value_block = lax.dynamic_slice_in_dim(values_all, offset, block_len, 1)
            key_pos = offset + jnp.arange(block_len, dtype=jnp.int32)
            key_seg = lax.dynamic_slice_in_dim(seg_rows, offset, block_len, 1)
            part_q, part_k, part_v = pair_grads(
                queries,
                grad_attn,
                lse,
                delta,
                query_pos,
                query_seg,
                key_block,
                value_block,
                key_pos,
                key_seg,
            )
            return (carry + part_q, jnp.concatenate([part_k, part_v], axis=-1))

        grad_q, terms = lax.scan(back_keys, jnp.zeros(queries.shape, jnp.float32), block_ids)
        terms = jnp.moveaxis(terms, 0, 1).reshape(seq_count, length, HEADS, 2 * HEAD_DIM)
        owned_terms = lax.psum_scatter(terms, "ctx", scatter_dimension=1, tiled=True)
        grad_k = owned_terms[..., :HEAD_DIM]
        grad_v = owned_terms[..., HEAD_DIM:]
        grad_qkv = jnp.concatenate(
            [
                grad_q.reshape(row_count, width),
                grad_k.reshape(row_count, width),
                grad_v.reshape(row_count, width),
            ],
            axis=-1,
        ).astype(jnp.bfloat16)
        grad_qkvw = matmul_left_t(norm_a, grad_qkv)
        grad_norm_a = matmul_right_t(grad_qkv, qkv_full)
        _, pull_one = jax.vjp(crms, inputs, gain_one.astype(jnp.float32))
        grad_input_norm, grad_gain_one = pull_one(grad_norm_a)
        grad_inputs = (grad_mixed + grad_input_norm).reshape(seq_count, local_len, res_width)
        return (
            grad_inputs,
            (grad_qkvw, grad_outw, grad_up, grad_down, grad_gain_one, grad_gain_two),
        )

    outputs = []
    input_grads = []
    owned = None
    for number in range(micro_count):
        (
            forward_qkv_full,
            forward_out_full,
            forward_up_full,
            forward_down_full,
            forward_gain_one,
            forward_gain_two,
        ) = fetch()
        forward_width = forward_qkv_full.shape[0]
        forward_inputs = tokens[number].astype(jnp.float32).reshape(row_count, res_width)
        forward_seg_rows = segment_ids[number]
        forward_query_seg = lax.dynamic_slice_in_dim(forward_seg_rows, first, local_len, 1)
        forward_norm_a = crms(forward_inputs, forward_gain_one.astype(jnp.float32)).astype(
            jnp.bfloat16
        )
        qkv = matmul(forward_norm_a, forward_qkv_full).astype(jnp.bfloat16)
        forward_queries = qkv[:, :forward_width].reshape(seq_count, local_len, HEADS, HEAD_DIM)
        forward_keys_own = qkv[:, forward_width : 2 * forward_width].reshape(
            seq_count, local_len, HEADS, HEAD_DIM
        )
        forward_values_own = qkv[:, 2 * forward_width :].reshape(
            seq_count, local_len, HEADS, HEAD_DIM
        )

        def fold_keys(state, piece):
            keys_part, values_part = piece
            span = keys_part.shape[1]
            block_len = span if span <= 1024 else math.gcd(span, 1024)

            def inner(carry, number_block):
                offset = number_block * block_len
                key_block = lax.dynamic_slice_in_dim(keys_part, offset, block_len, 1)
                value_block = lax.dynamic_slice_in_dim(values_part, offset, block_len, 1)
                key_pos = offset + jnp.arange(block_len, dtype=jnp.int32)
                key_seg = lax.dynamic_slice_in_dim(forward_seg_rows, offset, block_len, 1)
                return (
                    attend_block(
                        carry,
                        forward_queries,
                        query_pos,
                        forward_query_seg,
                        key_block,
                        value_block,
                        key_pos,
                        key_seg,
                    ),
                    None,
                )

            state, _ = lax.scan(inner, state, jnp.arange(span // block_len, dtype=jnp.int32))
            return state

        initial = (
            jnp.full((seq_count, HEADS, local_len), NEG, jnp.float32),
            jnp.zeros((seq_count, HEADS, local_len), jnp.float32),
            jnp.zeros((seq_count, HEADS, local_len, HEAD_DIM), jnp.float32),
        )
        best, denom, accum = fold_keys(
            initial,
            (
                lax.all_gather(forward_keys_own, "ctx", axis=1, tiled=True),
                lax.all_gather(forward_values_own, "ctx", axis=1, tiled=True),
            ),
        )
        heads_out = accum / denom[..., None]
        forward_lse = best + jnp.log(denom)
        forward_attn_f32 = jnp.transpose(heads_out, (0, 2, 1, 3))
        forward_attn = forward_attn_f32.reshape(row_count, forward_width).astype(jnp.bfloat16)
        forward_mixed = forward_inputs + matmul(forward_attn, forward_out_full)
        forward_norm_m = crms(forward_mixed, forward_gain_two.astype(jnp.float32)).astype(
            jnp.bfloat16
        )
        forward_pre = matmul(forward_norm_m, forward_up_full)
        forward_act = gelu_tanh(forward_pre).astype(jnp.bfloat16)
        result = (forward_mixed + matmul(forward_act, forward_down_full)).reshape(
            seq_count, local_len, res_width
        )
        forward_saved = (
            forward_inputs,
            forward_seg_rows,
            forward_query_seg,
            forward_norm_a,
            forward_queries,
            forward_keys_own,
            forward_values_own,
            forward_attn_f32,
            forward_lse,
            forward_attn,
            forward_mixed,
            forward_norm_m,
            forward_pre,
            forward_act,
        )
        result, saved = (result, forward_saved)
        grad_inputs, grads = backward(number, fetch(), saved)
        outputs.append(result)
        input_grads.append(grad_inputs)
        shares = (
            lax.psum_scatter(grads[0], ("seq", "ctx"), scatter_dimension=0, tiled=True),
            lax.psum_scatter(grads[1], ("seq", "ctx"), scatter_dimension=0, tiled=True),
            lax.psum_scatter(grads[2], ("seq", "ctx"), scatter_dimension=0, tiled=True),
            lax.psum_scatter(grads[3], ("seq", "ctx"), scatter_dimension=0, tiled=True),
            lax.psum_scatter(grads[4], ("seq", "ctx"), scatter_dimension=0, tiled=True),
            lax.psum_scatter(grads[5], ("seq", "ctx"), scatter_dimension=0, tiled=True),
        )
        owned = shares if owned is None else jax.tree.map(jnp.add, owned, shares)
    return (jnp.stack(outputs), jnp.stack(input_grads)) + tuple(owned)


def solution(mesh):
    return jax.shard_map(
        body,
        mesh=mesh,
        in_specs=(
            P(None, "seq", "ctx", None),
            P(None, "seq", None),
            P(("seq", "ctx"), None),
            P(("seq", "ctx"), None),
            P(("seq", "ctx"), None),
            P(("seq", "ctx"), None),
            P(("seq", "ctx")),
            P(("seq", "ctx")),
            P(None, "seq", "ctx", None),
        ),
        out_specs=(
            P(None, "seq", "ctx", None),
            P(None, "seq", "ctx", None),
            P(("seq", "ctx"), None),
            P(("seq", "ctx"), None),
            P(("seq", "ctx"), None),
            P(("seq", "ctx"), None),
            P(("seq", "ctx")),
            P(("seq", "ctx")),
        ),
        check_vma=False,
    )
```

profile of v0, /device:TPU:0, one launch (start us, length us, event | category | flops | bytes accessed | tf_op | source)
XLA Modules:
  0.0 1496.1 jit_solution(17649437479589515464)
XLA Ops:
  10.4 42.3 %all-reduce.5 = (bf16[768]{0:T(1024)(128)(2,1)S(1)}, bf16[768]{0:T(1024)(128)(2,1)S(1)}) all-reduce(bf16[768]{0:T(1024)(128)(2,1)S(1)} %dynamic-update-slice, bf16[768]{0:T(1024)(128)(2,1)S(1)} %dynamic-update-slice.1), channel_id=1, replica_groups=mesh['seq'=4,'ctx'=8] {'seq','ctx'}, use_global_device_ids=true, to_apply=%add | all-reduce | flops 1536 | bytes 6144
  53.6 20.3 %all-gather.11.cloned.1.call-done = bf16[768,2304]{1,0:T(8,128)(2,1)} async-done(((bf16[24,2304]{1,0:T(8,128)(2,1)}), bf16[768,2304]{1,0:T(8,128)(2,1)}) %all-gather.11.cloned.1.call-update) | async-done | bytes 3538960 | tf_op jit(solution)/shard_map/all_gather | solution.py:103
  73.9 2.8 convolution_convert_fusion
  78.3 2.1 copy.283
  82.3 2.0 copy.286
  93.1 2.0 copy.273
  96.9 2.0 copy.276
  116.3 23.6 %all-gather.27.cloned.1.call-done = bf16[1,768,12,64]{3,2,0,1:T(8,128)(2,1)} async-done(((bf16[1,96,12,64]{3,2,0,1:T(8,128)(2,1)}), bf16[1,768,12,64]{3,2,0,1:T(8,128)(2,1)}) %all-gather.27.cloned.1.call-update) | async-done | bytes 1179664 | tf_op jit(solution)/shard_map/all_gather | solution.py:262
  139.9 4.6 copy.284
  144.5 57.3 %all-gather.29.cloned.1.call-done = bf16[1,768,12,64]{3,2,0,1:T(8,128)(2,1)} async-done(((bf16[1,96,12,64]{3,2,0,1:T(8,128)(2,1)}), bf16[1,768,12,64]{3,2,0,1:T(8,128)(2,1)}) %all-gather.29.cloned.1.call-update) | async-done | bytes 1179664 | tf_op jit(solution)/shard_map/all_gather | solution.py:263
  201.8 4.6 copy.287
  206.4 56.5 %all-gather.23.cloned.1.call-done = bf16[1,768,12,64]{3,2,0,1:T(8,128)(2,1)} async-done(((bf16[1,96,12,64]{3,2,0,1:T(8,128)(2,1)}), bf16[1,768,12,64]{3,2,0,1:T(8,128)(2,1)}) %all-gather.23.cloned.1.call-update) | async-done | bytes 1179664 | tf_op jit(solution)/shard_map/all_gather | solution.py:262
  262.9 4.7 copy.274
  267.6 56.5 %all-gather.25.cloned.1.call-done = bf16[1,768,12,64]{3,2,0,1:T(8,128)(2,1)} async-done(((bf16[1,96,12,64]{3,2,0,1:T(8,128)(2,1)}), bf16[1,768,12,64]{3,2,0,1:T(8,128)(2,1)}) %all-gather.25.cloned.1.call-update) | async-done | bytes 1179664 | tf_op jit(solution)/shard_map/all_gather | solution.py:263
  324.1 4.6 copy.277
  328.6 56.6 %all-gather.13.cloned.1.call-done = bf16[1,768,12,64]{3,2,0,1:T(8,128)(2,1)} async-done(((bf16[1,96,12,64]{3,2,0,1:T(8,128)(2,1)}), bf16[1,768,12,64]{3,2,0,1:T(8,128)(2,1)}) %all-gather.13.cloned.1.call-update) | async-done | bytes 1179664 | tf_op jit(solution)/shard_map/all_gather | solution.py:262
  385.2 4.6 copy.264
  389.8 56.7 %all-gather.15.cloned.1.call-done = bf16[1,768,12,64]{3,2,0,1:T(8,128)(2,1)} async-done(((bf16[1,96,12,64]{3,2,0,1:T(8,128)(2,1)}), bf16[1,768,12,64]{3,2,0,1:T(8,128)(2,1)}) %all-gather.15.cloned.1.call-update) | async-done | bytes 1179664 | tf_op jit(solution)/shard_map/all_gather | solution.py:263
  446.5 4.6 copy.267
  451.1 2.2 fusion.80
  454.4 3.4 fusion.307
  457.8 44.4 %all-gather.17.cloned.1.call-done = bf16[768,767]{1,0:T(8,128)(2,1)} async-done(((bf16[24,767]{1,0:T(8,128)(2,1)}), bf16[768,767]{1,0:T(8,128)(2,1)}) %all-gather.17.cloned.1.call-update) | async-done | bytes 1178128 | tf_op jit(solution)/shard_map/all_gather | solution.py:104
  504.1 2.3 fusion.79
  507.6 3.4 fusion.308
  511.7 2.2 fusion.78
  515.1 3.4 fusion.309
  519.9 47.9 %all-gather.19.cloned.1.call-done = bf16[768,3072]{1,0:T(8,128)(2,1)} async-done(((bf16[24,3072]{1,0:T(8,128)(2,1)}), bf16[768,3072]{1,0:T(8,128)(2,1)}) %all-gather.19.cloned.1.call-update) | async-done | bytes 4718608 | tf_op jit(solution)/shard_map/all_gather | solution.py:105
  567.8 4.3 fusion.298
  572.1 60.9 %all-gather.21.cloned.1.call-done = bf16[3072,767]{1,0:T(8,128)(2,1)} async-done(((bf16[96,767]{1,0:T(8,128)(2,1)}), bf16[3072,767]{1,0:T(8,128)(2,1)}) %all-gather.21.cloned.1.call-update) | async-done | bytes 4712464 | tf_op jit(solution)/shard_map/all_gather | solution.py:106
  633.0 4.9 fusion.128
  646.4 3.0 multiply_reduce_fusion.2
  650.7 2.7 broadcast.914.clone2
  653.5 31.2 %while.11 = (s32[]{:T(128)}, f32[1,96,12,64]{1,3,2,0:T(8,128)}, f32[3,1,256,12,128]{4,2,0,3,1:T(8,128)}, s32[3]{0:T(128)S(1)}, bf16[1,768,12,64]{1,3,2,0:T(8,128...) while((s32[]{:T(128)}, f32[1,96,12,64]{1,3,2,0:T(8,128)}, ...), condition=%wide.region_33.34_spmd.clone, body=%wide.region_32.33_spmd.clone.sunk | while | flops 191693152 | bytes 18910308 | solution.py:175
  658.4 2.1 fusion.439
  668.6 2.2 fusion.439
  679.1 2.2 fusion.439
  689.0 2.8 broadcast.914.clone2.1
  691.7 31.4 %while.10 = (s32[]{:T(128)}, f32[1,96,12,64]{1,3,2,0:T(8,128)}, f32[3,1,256,12,128]{4,2,0,3,1:T(8,128)}, s32[3]{0:T(128)S(1)}, bf16[1,768,12,64]{1,3,2,0:T(8,128...) while((s32[]{:T(128)}, f32[1,96,12,64]{1,3,2,0:T(8,128)}, ...), condition=%wide.region_27.28_spmd.clone, body=%wide.region_26.27_spmd.clone.sunk | while | flops 191693152 | bytes 18895424 | solution.py:175
  696.7 2.1 fusion.425
  707.0 2.2 fusion.425
  717.5 2.2 fusion.425
  725.3 2.7 broadcast.914.clone2.2
  727.9 26.4 %while.9 = (s32[]{:T(128)}, f32[1,96,12,64]{1,3,2,0:T(8,128)}, f32[3,1,256,12,128]{4,2,0,3,1:T(8,128)}, s32[3]{0:T(128)S(1)}, bf16[1,768,12,64]{1,3,2,0:T(8,128)...) while((s32[]{:T(128)}, f32[1,96,12,64]{1,3,2,0:T(8,128)}, ...), condition=%wide.region_21.22_spmd.clone, body=%wide.region_20.21_spmd.clone.sunk | while | flops 191693152 | bytes 18846272 | solution.py:175
  732.2 2.1 fusion.411
  740.9 2.2 fusion.411
  749.7 2.2 fusion.411
  757.1 1.9 add_add_fusion.3
  763.3 5.4 add_add_fusion
  769.7 2.6 fusion.294
  773.8 5.0 add_add_fusion.1
  788.8 89.0 %reduce-scatter.10.cloned.1.call-done = f32[1,96,12,128]{3,1,2,0:T(8,128)} async-done(((f32[1,768,12,128]{3,1,2,0:T(8,128)}), f32[1,96,12,128]{3,1,2,0:T(8,128)}) %reduce-scatter.10.cloned.1.call-update) | async-done | bytes 589840 | tf_op jit(solution)/shard_map/reduce_scatter | solution.py:177
  882.3 94.1 %reduce-scatter.8.cloned.1.call-done = f32[1,96,12,128]{3,1,2,0:T(8,128)} async-done(((f32[1,768,12,128]{3,1,2,0:T(8,128)}), f32[1,96,12,128]{3,1,2,0:T(8,128)}) %reduce-scatter.8.cloned.1.call-update) | async-done | bytes 589840 | tf_op jit(solution)/shard_map/reduce_scatter | solution.py:177
  982.1 2.3 fusion.189
  985.7 4.1 add_add_fusion.2
  989.9 4.2 fusion.96
  994.2 4.3 fusion.97
  998.6 4.4 fusion.98
  1004.0 2.6 copy.326
  1007.2 2.3 fusion.186
  1015.4 40.5 %all-reduce.4 = (f32[768]{0:T(1024)S(1)}, f32[768]{0:T(1024)S(1)}) all-reduce(f32[768]{0:T(1024)S(1)} %add_add_fusion.11, f32[768]{0:T(1024)S(1)} %copy-done.101), channel_id=21, replica_groups=mesh['seq'=4,'ctx'=8] {'seq','ctx'}, use_global_device_ids=true, to_apply=%region_49.50.clone | all-reduce | flops 1536 | bytes 12288
  1057.0 24.0 %reduce-scatter.16.cloned.1.call-done = f32[24,767]{1,0:T(8,128)} async-done(((f32[768,767]{1,0:T(8,128)}), f32[24,767]{1,0:T(8,128)}) %reduce-scatter.16.cloned.1.call-update) | async-done | bytes 73648 | tf_op jit(solution)/shard_map/reduce_scatter | solution.py:301
  1081.0 142.0 %reduce-scatter.20.cloned.1.call-done = f32[96,767]{1,0:T(8,128)} async-done(((f32[3072,767]{1,0:T(8,128)}), f32[96,767]{1,0:T(8,128)}) %reduce-scatter.20.cloned.1.call-update) | async-done | bytes 294544 | tf_op jit(solution)/shard_map/reduce_scatter | solution.py:303
  1223.1 140.9 %reduce-scatter.18.cloned.1.call-done = f32[24,3072]{1,0:T(8,128)} async-done(((f32[768,3072]{1,0:T(8,128)}), f32[24,3072]{1,0:T(8,128)}) %reduce-scatter.18.cloned.1.call-update) | async-done | bytes 294928 | tf_op jit(solution)/shard_map/reduce_scatter | solution.py:302
  1363.9 125.2 %reduce-scatter.14.cloned.1.call-done = f32[24,2304]{1,0:T(8,128)} async-done(((f32[768,2304]{1,0:T(8,128)}), f32[24,2304]{1,0:T(8,128)}) %reduce-scatter.14.cloned.1.call-update) | async-done | bytes 221200 | tf_op jit(solution)/shard_map/reduce_scatter | solution.py:300
  (674 shorter events, 159.2 us)
Async XLA Ops:
  7.2 3.0 copy-start.166
  7.2 66.7 %all-gather.11.cloned.1.call-start = ((), (), s32[]{:S(2)}) async-start(), calls=%async_computation.7 | async-start | bytes 3649536 | tf_op jit(solution)/shard_map/all_gather | solution.py:103
  7.9 132.0 %all-gather.27.cloned.1.call-start = ((), (), s32[]{:S(2)}) async-start(), calls=%async_computation.15 | async-start | bytes 3538944 | tf_op jit(solution)/shard_map/all_gather | solution.py:262
  9.9 66.8 %copy-start.20 = (bf16[1,1,96,767]{2,3,1,0:T(8,128)(2,1)}, bf16[1,1,96,767]{2,3,1,0:T(8,128)(2,1)S(1)}, u32[]{:S(2)}) copy-start(bf16[1,1,96,767]{2,3,1,0:T(8,128)(2,1)S(1)} %copy.348) | copy-start | bytes 441796
  52.7 51.6 %copy-start.75 = (f32[768]{0:T(1024)}, f32[768]{0:T(1024)S(1)}, u32[]{:S(2)}) copy-start(f32[768]{0:T(1024)S(1)} %convert_element_type.210) | copy-start | bytes 9220
  53.5 20.4 %copy-start.153 = (f32[96,1]{0,1:T(1,128)}, f32[96,1]{0,1:T(1,128)S(1)}, u32[]{:S(2)}) copy-start(f32[96,1]{0,1:T(1,128)S(1)} %bitcast_negate_fusion.1) | copy-start | bytes 1156
  53.5 20.4 %copy-start.156 = (f32[96]{0:T(128)}, f32[96]{0:T(128)S(1)}, u32[]{:S(2)}) copy-start(f32[96]{0:T(128)S(1)} %fusion.283) | copy-start | bytes 1156
  53.6 23.2 %copy-start.43 = (f32[96,767]{0,1:T(8,128)}, f32[96,767]{0,1:T(8,128)S(1)}, u32[]{:S(2)}) copy-start(f32[96,767]{0,1:T(8,128)S(1)} %convert_bitcast_fusion) | copy-start | bytes 883588
  78.3 11.4 copy-start.4
  80.5 121.3 %all-gather.29.cloned.1.call-start = ((), (), s32[]{:S(2)}) async-start(), calls=%async_computation.16 | async-start | bytes 3538944 | tf_op jit(solution)/shard_map/all_gather | solution.py:263
  84.3 178.6 %all-gather.23.cloned.1.call-start = ((), (), s32[]{:S(2)}) async-start(), calls=%async_computation.13 | async-start | bytes 3538944 | tf_op jit(solution)/shard_map/all_gather | solution.py:262
  95.1 229.0 %all-gather.25.cloned.1.call-start = ((), (), s32[]{:S(2)}) async-start(), calls=%async_computation.14 | async-start | bytes 3538944 | tf_op jit(solution)/shard_map/all_gather | solution.py:263
  98.9 286.3 %all-gather.13.cloned.1.call-start = ((), (), s32[]{:S(2)}) async-start(), calls=%async_computation.8 | async-start | bytes 3538944 | tf_op jit(solution)/shard_map/all_gather | solution.py:262
  106.4 3.7 copy-start.51
  106.5 340.0 %all-gather.15.cloned.1.call-start = ((), (), s32[]{:S(2)}) async-start(), calls=%async_computation.9 | async-start | bytes 3538944 | tf_op jit(solution)/shard_map/all_gather | solution.py:263
  106.7 5.1 copy-start.102
  107.8 6.7 copy-start.79
  107.8 7.5 copy-start.80
  107.8 394.4 %all-gather.17.cloned.1.call-start = ((), (), s32[]{:S(2)}) async-start(), calls=%async_computation.10 | async-start | bytes 1216512 | tf_op jit(solution)/shard_map/all_gather | solution.py:104
  108.6 459.2 %all-gather.19.cloned.1.call-start = ((), (), s32[]{:S(2)}) async-start(), calls=%async_computation.11 | async-start | bytes 4866048 | tf_op jit(solution)/shard_map/all_gather | solution.py:105
  109.3 523.7 %all-gather.21.cloned.1.call-start = ((), (), s32[]{:S(2)}) async-start(), calls=%async_computation.12 | async-start | bytes 4866048 | tf_op jit(solution)/shard_map/all_gather | solution.py:106
  109.9 674.3 %reduce-scatter.12.cloned.1.call-start = ((), (), s32[]{:S(2)}) async-start(), calls=%async_computation.19 | async-start | bytes 5308416 | tf_op jit(solution)/shard_map/reduce_scatter | solution.py:177
  454.4 47.8 %copy-start.21 = (bf16[1,1,96,767]{2,3,1,0:T(8,128)(2,1)S(1)}, bf16[1,1,96,767]{2,3,1,0:T(8,128)(2,1)}, u32[]{:S(2)}) copy-start(bf16[1,1,96,767]{2,3,1,0:T(8,128)(2,1)} %copy-done.20) | copy-start | bytes 441796
  457.8 48.7 %copy-start.73 = (bf16[1,96,12,64]{1,3,2,0:T(8,128)(2,1)}, bf16[1,96,12,64]{1,3,2,0:T(8,128)(2,1)S(1)}, u32[]{:S(2)}) copy-start(bf16[1,96,12,64]{1,3,2,0:T(8,128)(2,1)S(1)} %get-tuple-element.733) | copy-start | bytes 442372
  504.1 15.0 %copy-start.149 = (f32[96]{0:T(128)}, f32[96]{0:T(128)S(1)}, u32[]{:S(2)}) copy-start(f32[96]{0:T(128)S(1)} %get-tuple-element.584) | copy-start | bytes 1156
  504.1 15.0 %copy-start.151 = (f32[96]{0:T(128)}, f32[96]{0:T(128)S(1)}, u32[]{:S(2)}) copy-start(f32[96]{0:T(128)S(1)} %get-tuple-element.585) | copy-start | bytes 1156
  504.1 145.3 %copy-start.6 = (f32[96,767]{0,1:T(8,128)}, f32[96,767]{0,1:T(8,128)S(1)}, u32[]{:S(2)}) copy-start(f32[96,767]{0,1:T(8,128)S(1)} %get-tuple-element.735) | copy-start | bytes 883588
  504.1 63.6 %copy-start.115 = (f32[96,1]{0,1:T(1,128)}, f32[96,1]{0,1:T(1,128)S(1)}, u32[]{:S(2)}) copy-start(f32[96,1]{0,1:T(1,128)S(1)} %bitcast_negate_fusion) | copy-start | bytes 1156
  507.6 3.5 copy-start.90
  507.6 3.5 copy-start.1
  507.6 3.5 copy-start.23
  511.7 7.5 copy-start.139
  511.7 7.5 copy-start.141
  511.7 134.5 %copy-start.8 = (f32[96,767]{0,1:T(8,128)}, f32[96,767]{0,1:T(8,128)S(1)}, u32[]{:S(2)}) copy-start(f32[96,767]{0,1:T(8,128)S(1)} %get-tuple-element.740) | copy-start | bytes 883588
  511.7 127.7 %copy-start.118 = (f32[96,1]{0,1:T(1,128)}, f32[96,1]{0,1:T(1,128)S(1)}, u32[]{:S(2)}) copy-start(f32[96,1]{0,1:T(1,128)S(1)} %bitcast_negate_fusion.2) | copy-start | bytes 1156
  515.1 3.4 copy-start.88
  515.1 3.4 copy-start.25
  518.5 53.6 %copy-start.61 = (bf16[1,96,12,64]{1,3,2,0:T(8,128)(2,1)}, bf16[1,96,12,64]{1,3,2,0:T(8,128)(2,1)S(1)}, u32[]{:S(2)}) copy-start(bf16[1,96,12,64]{1,3,2,0:T(8,128)(2,1)S(1)} %get-tuple-element.743) | copy-start | bytes 442372
  519.1 53.0 %copy-start.143 = (f32[96]{0:T(128)}, f32[96]{0:T(128)S(1)}, u32[]{:S(2)}) copy-start(f32[96]{0:T(128)S(1)} %get-tuple-element.580) | copy-start | bytes 1156
  519.1 53.0 %copy-start.145 = (f32[96]{0:T(128)}, f32[96]{0:T(128)S(1)}, u32[]{:S(2)}) copy-start(f32[96]{0:T(128)S(1)} %get-tuple-element.581) | copy-start | bytes 1156
  519.1 127.1 %copy-start.11 = (f32[96,767]{0,1:T(8,128)}, f32[96,767]{0,1:T(8,128)S(1)}, u32[]{:S(2)}) copy-start(f32[96,767]{0,1:T(8,128)S(1)} %get-tuple-element.745) | copy-start | bytes 883588
  519.1 124.4 %copy-start.124 = (f32[96,1]{0,1:T(1,128)}, f32[96,1]{0,1:T(1,128)S(1)}, u32[]{:S(2)}) copy-start(f32[96,1]{0,1:T(1,128)S(1)} %bitcast_negate_fusion.4) | copy-start | bytes 1156
  519.2 53.0 %copy-start.121 = (f32[96]{0:T(128)}, f32[96]{0:T(128)S(1)}, u32[]{:S(2)}) copy-start(f32[96]{0:T(128)S(1)} %fusion.284) | copy-start | bytes 1156
  519.2 127.0 %copy-start.103 = (f32[96]{0:T(128)}, f32[96]{0:T(128)S(1)}, u32[]{:S(2)}) copy-start(f32[96]{0:T(128)S(1)} %fusion.282) | copy-start | bytes 1156
  519.2 127.0 %copy-start.105 = (f32[96]{0:T(128)}, f32[96]{0:T(128)S(1)}, u32[]{:S(2)}) copy-start(f32[96]{0:T(128)S(1)} %fusion.280) | copy-start | bytes 1156
  633.0 4.9 copy-start
  633.0 7.4 slice-start
  646.3 3.0 copy-start.63
  684.8 192.9 %reduce-scatter.10.cloned.1.call-start = ((), (), s32[]{:S(2)}) async-start(), calls=%async_computation.18 | async-start | bytes 5308416 | tf_op jit(solution)/shard_map/reduce_scatter | solution.py:177
  723.1 253.3 %reduce-scatter.8.cloned.1.call-start = ((), (), s32[]{:S(2)}) async-start(), calls=%async_computation.17 | async-start | bytes 5308416 | tf_op jit(solution)/shard_map/reduce_scatter | solution.py:177
  754.4 326.7 %reduce-scatter.16.cloned.1.call-start = ((), (), s32[]{:S(2)}) async-start(), calls=%async_computation.21 | async-start | bytes 2433024 | tf_op jit(solution)/shard_map/reduce_scatter | solution.py:301
  759.0 464.0 %reduce-scatter.20.cloned.1.call-start = ((), (), s32[]{:S(2)}) async-start(), calls=%async_computation.23 | async-start | bytes 9732096 | tf_op jit(solution)/shard_map/reduce_scatter | solution.py:303
  768.7 3.6 copy-start.10
  768.7 3.6 copy-start.104
  768.7 3.6 copy-start.120
  768.8 595.2 %reduce-scatter.18.cloned.1.call-start = ((), (), s32[]{:S(2)}) async-start(), calls=%async_computation.22 | async-start | bytes 9732096 | tf_op jit(solution)/shard_map/reduce_scatter | solution.py:302
  778.8 710.3 %reduce-scatter.14.cloned.1.call-start = ((), (), s32[]{:S(2)}) async-start(), calls=%async_computation.20 | async-start | bytes 7299072 | tf_op jit(solution)/shard_map/reduce_scatter | solution.py:300
  977.5 4.5 copy-start.41
  977.5 4.5 copy-start.76
  977.5 4.5 copy-start.113
  977.6 4.5 copy-start.163
  994.2 4.4 copy-start.14
  994.2 4.4 copy-start.19
  998.6 8.7 copy-start.5
  (148 other events, 228.8 us)
Sparse Core Ops, SparseCore 0:
  10.9 62.9 all-gather.10
  80.6 59.2 all-gather.26
  142.7 59.0 all-gather.28
  203.8 59.0 all-gather.22
  265.0 59.0 all-gather.24
  326.1 59.0 all-gather.12
  387.4 59.0 all-gather.14
  449.4 52.7 all-gather.16
  505.2 62.5 all-gather.18
  570.5 62.4 all-gather.20
  684.9 94.0 reduce-scatter.11
  782.5 95.1 reduce-scatter.9
  881.4 94.9 reduce-scatter.7
  982.1 98.8 reduce-scatter.15
  1088.4 134.6 reduce-scatter.19
  1229.4 134.4 reduce-scatter.17
  1371.0 118.1 reduce-scatter.13
where the time goes:
time: 1500 us
  waiting for transfers between devices  1100 us (73%)
  matrix products  147 us (10%)
  local copies, waits for them, and re-layouts  117 us (8%)
  blocking collectives  82.7 us (6%)
  other arithmetic  25.5 us (2%)
  between operations  17 us (1%)
    reduce_scatter x3, waiting for transfers between devices, backward(): lax.psum_scatter(terms, 'ctx', scatter_dimension=1, tiled=True)  183 us
    all_gather x3, waiting for transfers between devices, body(): lax.all_gather(forward_values_own, 'ctx', axis=1, tiled=True)  170 us
    reduce_scatter x1, waiting for transfers between devices, body(): lax.psum_scatter(grads[3], ('seq', 'ctx'), scatter_dimension=0, tiled=True)  142 us
    reduce_scatter x1, waiting for transfers between devices, body(): lax.psum_scatter(grads[2], ('seq', 'ctx'), scatter_dimension=0, tiled=True)  141 us
    all_gather x3, waiting for transfers between devices, body(): lax.all_gather(forward_keys_own, 'ctx', axis=1, tiled=True)  137 us
    reduce_scatter x1, waiting for transfers between devices, body(): lax.psum_scatter(grads[0], ('seq', 'ctx'), scatter_dimension=0, tiled=True)  125 us
    unnamed x2, blocking collectives  82.7 us
    all_gather x1, waiting for transfers between devices, fetch(): lax.all_gather(down_weight, ('seq', 'ctx'), axis=0, tiled=True)  60.9 us
  transfers between devices with their start and end apart: 17, of which 16 were waited for; matrix products, arithmetic and copies ran while one was open for 15% of the time, Pallas kernels for 0%

commit v1 on v0

--- a/solution.py
+++ b/solution.py
@@ -9,6 +9,27 @@
 EPS = 1e-05
 NEG = -1e30
 SCALE = 0.125
+
+
+def gather_around(array, axis, dim):
+    size, here, width = (lax.axis_size(axis), lax.axis_index(axis), array.shape[dim])
+    right = [(i, (i + 1) % size) for i in range(size)]
+    downward = [(i, (i - 1) % size) for i in range(size)]
+    whole = jnp.zeros((*array.shape[:dim], size * width, *array.shape[dim + 1 :]), array.dtype)
+    whole = lax.dynamic_update_slice_in_dim(whole, array, here * width, axis=dim)
+    from_left = from_right = array
+    half = size // 2
+    for step in range(1, half + 1):
+        from_left = lax.ppermute(from_left, axis, right)
+        whole = lax.dynamic_update_slice_in_dim(
+            whole, from_left, (here - step) % size * width, axis=dim
+        )
+        if step < size - half:
+            from_right = lax.ppermute(from_right, axis, downward)
+            whole = lax.dynamic_update_slice_in_dim(
+                whole, from_right, (here + step) % size * width, axis=dim
+            )
+    return whole
 
 
 def crms(inputs, gains):
@@ -260,7 +281,7 @@
             initial,
             (
                 lax.all_gather(forward_keys_own, "ctx", axis=1, tiled=True),
-                lax.all_gather(forward_values_own, "ctx", axis=1, tiled=True),
+                gather_around(forward_values_own, "ctx", 1),
             ),
         )
         heads_out = accum / denom[..., None]

time: 1500 us -> 1520 us (1.013)
  waiting for transfers between devices: 1100 us -> 980 us
  local copies, waits for them, and re-layouts: 117 us -> 214 us
  starting transfers between devices: 1.54 us -> 32.2 us
    dynamic_update_slice x0 -> x24, local copies, waits for them, and re-layouts: none -> 98.3 us  [the longest x12 53.5 us: gather_around(): lax.dynamic_update_slice_in_dim(whole, from_left, (here - step) % size *...]
    all_gather x3, waiting for transfers between devices: 137 us -> 41.5 us  [body(): lax.all_gather(forward_keys_own, 'ctx', axis=1, tiled=True)]
    all_gather x3, waiting for transfers between devices: 170 us -> 77.7 us  [backward(): lax.all_gather(values_own, 'ctx', axis=1, tiled=True)]
    ppermute x0 -> x21, waiting for transfers between devices: none -> 62.8 us  [the longest x9 41.7 us: gather_around(): from_right = lax.ppermute(from_right, axis, downward)]
    all_gather x1, waiting for transfers between devices: 44.4 us -> 0.01 us  [fetch(): lax.all_gather(out_weight, ('seq', 'ctx'), axis=0, tiled=True)]
    reduce_scatter x3, waiting for transfers between devices: 183 us -> 221 us  [backward(): lax.psum_scatter(terms, 'ctx', scatter_dimension=1, tiled=True)]
    ppermute x0 -> x21, starting transfers between devices: none -> 31 us  [the longest x9 21.9 us: gather_around(): from_right = lax.ppermute(from_right, axis, downward)]
    unnamed x344 -> x397, local copies, waits for them, and re-layouts: 19.2 us -> 32.9 us
  transfers between devices with their start and end apart: 17 -> 38, of which waited for: 16 -> 28; matrix products, arithmetic and copies ran while one was open for 15% -> 24% of each run, Pallas kernels for 0% -> 0%
where the time goes in v1:
time: 1520 us; the launch traced here: 1500 us
  waiting for transfers between devices  980 us (64%)
  local copies, waits for them, and re-layouts  214 us (14%)
  matrix products  143 us (9%)
  blocking collectives  82.8 us (5%)
  starting transfers between devices  32.2 us (2%)
  other arithmetic  28.4 us (2%)
  between operations  17.3 us (1%)
    reduce_scatter x3, waiting for transfers between devices, backward(): lax.psum_scatter(terms, 'ctx', scatter_dimension=1, tiled=True)  221 us
    reduce_scatter x1, waiting for transfers between devices, body(): lax.psum_scatter(grads[3], ('seq', 'ctx'), scatter_dimension=0, tiled=True)  142 us
    reduce_scatter x1, waiting for transfers between devices, body(): lax.psum_scatter(grads[2], ('seq', 'ctx'), scatter_dimension=0, tiled=True)  141 us
    reduce_scatter x1, waiting for transfers between devices, body(): lax.psum_scatter(grads[0], ('seq', 'ctx'), scatter_dimension=0, tiled=True)  125 us
    unnamed x2, blocking collectives  82.8 us
    all_gather x3, waiting for transfers between devices, backward(): lax.all_gather(values_own, 'ctx', axis=1, tiled=True)  77.7 us
    all_gather x1, waiting for transfers between devices, fetch(): lax.all_gather(down_weight, ('seq', 'ctx'), axis=0, tiled=True)  61.1 us
    all_gather x1, waiting for transfers between devices, fetch(): lax.all_gather(up_weight, ('seq', 'ctx'), axis=0, tiled=True)  60.6 us
  transfers between devices with their start and end apart: 38, of which 28 were waited for; matrix products, arithmetic and copies ran while one was open for 24% of the time, Pallas kernels for 0%

profile of v1, /device:TPU:0, one launch (start us, length us, event | category | flops | bytes accessed | tf_op | source)
XLA Modules:
  0.0 1503.4 jit_solution(18432916350200224412)
XLA Ops:
  10.4 42.3 %all-reduce.5 = (bf16[768]{0:T(1024)(128)(2,1)S(1)}, bf16[768]{0:T(1024)(128)(2,1)}) all-reduce(bf16[768]{0:T(1024)(128)(2,1)S(1)} %dynamic-update-slice, bf16[768]{0:T(1024)(128)(2,1)S(1)} %dynamic-update-slice.1), channel_id=1, replica_groups=mesh['seq'=4,'ctx'=8] {'seq','ctx'}, use_global_device_ids=true, to_apply=%add | all-reduce | flops 1536 | bytes 6144
  53.6 20.3 %all-gather.11.cloned.1.call-done = bf16[768,2304]{1,0:T(8,128)(2,1)} async-done(((bf16[24,2304]{1,0:T(8,128)(2,1)}), bf16[768,2304]{1,0:T(8,128)(2,1)}) %all-gather.11.cloned.1.call-update) | async-done | bytes 3538960 | tf_op jit(solution)/shard_map/all_gather | solution.py:124
  110.6 4.7 collective-permute-start.8
  120.9 10.2 collective-permute-done.15
  131.1 6.0 collective-permute-done.7
  137.1 7.4 collective-permute-done.8
  144.5 3.5 collective-permute-done
  149.8 7.3 collective-permute-done.1
  162.4 7.3 collective-permute-done.17
  170.9 4.0 collective-permute-start.19
  183.5 3.8 collective-permute-start.5
  187.3 4.8 collective-permute-done.19
  196.6 3.7 collective-permute-done.4
  210.0 3.4 dynamic_update_slice.114
  215.3 3.4 dynamic_update_slice.123
  218.8 4.2 dynamic_update_slice.115
  222.9 3.6 dynamic_update_slice.124
  226.6 4.9 dynamic_update_slice.116
  231.5 3.4 dynamic_update_slice.107
  234.9 3.6 dynamic_update_slice.108
  238.5 3.6 dynamic_update_slice.125
  242.1 4.8 dynamic_update_slice.117
  246.9 3.6 dynamic_update_slice.126
  250.5 4.8 dynamic_update_slice.118
  255.2 3.6 dynamic_update_slice.109
  258.8 4.3 dynamic_update_slice.110
  263.1 4.2 dynamic_update_slice.127
  267.3 4.8 dynamic_update_slice.119
  272.1 4.2 dynamic_update_slice.128
  276.4 4.8 dynamic_update_slice.120
  281.2 12.7 dynamic_update_slice.111
  293.9 4.3 dynamic_update_slice.112
  300.9 3.5 dynamic_update_slice.121
  307.1 5.0 copy.297
  321.2 4.7 copy.288
  333.1 41.4 %all-gather.13.cloned.1.call-done = bf16[1,768,12,64]{3,2,0,1:T(8,128)(2,1)} async-done(((bf16[1,96,12,64]{3,2,0,1:T(8,128)(2,1)}), bf16[1,768,12,64]{3,2,0,1:T(8,128)(2,1)}) %all-gather.13.cloned.1.call-update) | async-done | bytes 1179664 | tf_op jit(solution)/shard_map/all_gather | solution.py:283
  374.5 5.0 copy.279
  385.6 50.0 %all-gather.29.cloned.1.call-done = bf16[1,768,12,64]{3,2,0,1:T(8,128)(2,1)} async-done(((bf16[1,96,12,64]{3,2,0,1:T(8,128)(2,1)}), bf16[1,768,12,64]{3,2,0,1:T(8,128)(2,1)}) %all-gather.29.cloned.1.call-update) | async-done | bytes 1179664 | tf_op jit(solution)/shard_map/all_gather | solution.py:173
  435.6 4.6 copy.330
  440.3 60.6 %all-gather.17.cloned.1.call-done = bf16[768,3072]{1,0:T(8,128)(2,1)} async-done(((bf16[24,3072]{1,0:T(8,128)(2,1)}), bf16[768,3072]{1,0:T(8,128)(2,1)}) %all-gather.17.cloned.1.call-update) | async-done | bytes 4718608 | tf_op jit(solution)/shard_map/all_gather | solution.py:126
  500.9 4.4 fusion.283
  505.2 61.1 %all-gather.19.cloned.1.call-done = bf16[3072,767]{1,0:T(8,128)(2,1)} async-done(((bf16[96,767]{1,0:T(8,128)(2,1)}), bf16[3072,767]{1,0:T(8,128)(2,1)}) %all-gather.19.cloned.1.call-update) | async-done | bytes 4712464 | tf_op jit(solution)/shard_map/all_gather | solution.py:127
  566.3 4.5 fusion.128
  586.3 31.5 %while.11 = (s32[]{:T(128)}, f32[1,96,12,64]{1,3,2,0:T(8,128)}, f32[3,1,256,12,128]{4,2,0,3,1:T(8,128)}, s32[3]{0:T(128)S(1)}, bf16[1,768,12,64]{1,3,2,0:T(8,128...) while((s32[]{:T(128)}, f32[1,96,12,64]{1,3,2,0:T(8,128)}, ...), condition=%wide.region_33.34_spmd.clone, body=%wide.region_32.33_spmd.clone.sunk | while | flops 191693152 | bytes 18910308 | solution.py:196
  619.2 8.6 all-gather.27.cloned.1.call-done
  627.8 4.6 copy.319
  638.2 31.5 %while.10 = (s32[]{:T(128)}, f32[1,96,12,64]{1,3,2,0:T(8,128)}, f32[3,1,256,12,128]{4,2,0,3,1:T(8,128)}, s32[3]{0:T(128)S(1)}, bf16[1,768,12,64]{1,3,2,0:T(8,128...) while((s32[]{:T(128)}, f32[1,96,12,64]{1,3,2,0:T(8,128)}, ...), condition=%wide.region_27.28_spmd.clone, body=%wide.region_26.27_spmd.clone.sunk | while | flops 191693152 | bytes 18895424 | solution.py:196
  669.9 19.0 %all-gather.25.cloned.1.call-done = bf16[1,768,12,64]{3,2,0,1:T(8,128)(2,1)} async-done(((bf16[1,96,12,64]{3,2,0,1:T(8,128)(2,1)}), bf16[1,768,12,64]{3,2,0,1:T(8,128)(2,1)}) %all-gather.25.cloned.1.call-update) | async-done | bytes 1179664 | tf_op jit(solution)/shard_map/all_gather | solution.py:173
  688.9 4.6 copy.308
  697.7 26.4 %while.9 = (s32[]{:T(128)}, f32[1,96,12,64]{1,3,2,0:T(8,128)}, f32[3,1,256,12,128]{4,2,0,3,1:T(8,128)}, s32[3]{0:T(128)S(1)}, bf16[1,768,12,64]{1,3,2,0:T(8,128)...) while((s32[]{:T(128)}, f32[1,96,12,64]{1,3,2,0:T(8,128)}, ...), condition=%wide.region_21.22_spmd.clone, body=%wide.region_20.21_spmd.clone.sunk | while | flops 191693152 | bytes 18846272 | solution.py:196
  733.0 5.3 add_add_fusion
  743.4 5.0 add_add_fusion.1
  753.8 32.7 %reduce-scatter.12.cloned.1.call-done = f32[1,96,12,128]{3,1,2,0:T(8,128)} async-done(((f32[1,768,12,128]{3,1,2,0:T(8,128)}), f32[1,96,12,128]{3,1,2,0:T(8,128)}) %reduce-scatter.12.cloned.1.call-update) | async-done | bytes 589840 | tf_op jit(solution)/shard_map/reduce_scatter | solution.py:198
  791.1 94.0 %reduce-scatter.10.cloned.1.call-done = f32[1,96,12,128]{3,1,2,0:T(8,128)} async-done(((f32[1,768,12,128]{3,1,2,0:T(8,128)}), f32[1,96,12,128]{3,1,2,0:T(8,128)}) %reduce-scatter.10.cloned.1.call-update) | async-done | bytes 589840 | tf_op jit(solution)/shard_map/reduce_scatter | solution.py:198
  889.6 94.1 %reduce-scatter.8.cloned.1.call-done = f32[1,96,12,128]{3,1,2,0:T(8,128)} async-done(((f32[1,768,12,128]{3,1,2,0:T(8,128)}), f32[1,96,12,128]{3,1,2,0:T(8,128)}) %reduce-scatter.8.cloned.1.call-update) | async-done | bytes 589840 | tf_op jit(solution)/shard_map/reduce_scatter | solution.py:198
  993.1 4.1 add_add_fusion.2
  997.2 4.2 fusion.96
  1001.5 4.4 fusion.97
  1005.9 4.4 fusion.98
  1022.7 40.6 %all-reduce.4 = (f32[768]{0:T(1024)S(1)}, f32[768]{0:T(1024)S(1)}) all-reduce(f32[768]{0:T(1024)S(1)} %add_add_fusion.11, f32[768]{0:T(1024)S(1)} %copy-done.125), channel_id=21, replica_groups=mesh['seq'=4,'ctx'=8] {'seq','ctx'}, use_global_device_ids=true, to_apply=%region_49.50.clone | all-reduce | flops 1536 | bytes 12288
  1064.5 23.9 %reduce-scatter.16.cloned.1.call-done = f32[24,767]{1,0:T(8,128)} async-done(((f32[768,767]{1,0:T(8,128)}), f32[24,767]{1,0:T(8,128)}) %reduce-scatter.16.cloned.1.call-update) | async-done | bytes 73648 | tf_op jit(solution)/shard_map/reduce_scatter | solution.py:322
  1088.4 142.0 %reduce-scatter.20.cloned.1.call-done = f32[96,767]{1,0:T(8,128)} async-done(((f32[3072,767]{1,0:T(8,128)}), f32[96,767]{1,0:T(8,128)}) %reduce-scatter.20.cloned.1.call-update) | async-done | bytes 294544 | tf_op jit(solution)/shard_map/reduce_scatter | solution.py:324
  1230.4 140.9 %reduce-scatter.18.cloned.1.call-done = f32[24,3072]{1,0:T(8,128)} async-done(((f32[768,3072]{1,0:T(8,128)}), f32[24,3072]{1,0:T(8,128)}) %reduce-scatter.18.cloned.1.call-update) | async-done | bytes 294928 | tf_op jit(solution)/shard_map/reduce_scatter | solution.py:323
  1371.2 125.1 %reduce-scatter.14.cloned.1.call-done = f32[24,2304]{1,0:T(8,128)} async-done(((f32[768,2304]{1,0:T(8,128)}), f32[24,2304]{1,0:T(8,128)}) %reduce-scatter.14.cloned.1.call-update) | async-done | bytes 221200 | tf_op jit(solution)/shard_map/reduce_scatter | solution.py:321
  (793 shorter events, 265.6 us)
Async XLA Ops:
  7.2 66.7 %all-gather.11.cloned.1.call-start = ((), (), s32[]{:S(2)}) async-start(), calls=%async_computation.7 | async-start | bytes 3649536 | tf_op jit(solution)/shard_map/all_gather | solution.py:124
  7.9 299.2 %all-gather.23.cloned.1.call-start = ((), (), s32[]{:S(2)}) async-start(), calls=%async_computation.13 | async-start | bytes 3538944 | tf_op jit(solution)/shard_map/all_gather | solution.py:283
  9.9 64.0 %copy-start.20 = (bf16[1,1,96,767]{2,3,1,0:T(8,128)(2,1)}, bf16[1,1,96,767]{2,3,1,0:T(8,128)(2,1)S(1)}, u32[]{:S(2)}) copy-start(bf16[1,1,96,767]{2,3,1,0:T(8,128)(2,1)S(1)} %copy.363) | copy-start | bytes 441796
  81.7 236.3 %all-gather.15.cloned.1.call-start = ((), (), s32[]{:S(2)}) async-start(), calls=%async_computation.9 | async-start | bytes 1216512 | tf_op jit(solution)/shard_map/all_gather | solution.py:125
  82.5 238.8 %all-gather.21.cloned.1.call-start = ((), (), s32[]{:S(2)}) async-start(), calls=%async_computation.12 | async-start | bytes 3538944 | tf_op jit(solution)/shard_map/all_gather | solution.py:283
  93.2 281.3 %all-gather.13.cloned.1.call-start = ((), (), s32[]{:S(2)}) async-start(), calls=%async_computation.8 | async-start | bytes 3538944 | tf_op jit(solution)/shard_map/all_gather | solution.py:283
  100.8 334.8 %all-gather.29.cloned.1.call-start = ((), (), s32[]{:S(2)}) async-start(), calls=%async_computation.18 | async-start | bytes 3538944 | tf_op jit(solution)/shard_map/all_gather | solution.py:173
  102.2 398.7 %all-gather.17.cloned.1.call-start = ((), (), s32[]{:S(2)}) async-start(), calls=%async_computation.10 | async-start | bytes 4866048 | tf_op jit(solution)/shard_map/all_gather | solution.py:126
  102.9 463.4 %all-gather.19.cloned.1.call-start = ((), (), s32[]{:S(2)}) async-start(), calls=%async_computation.11 | async-start | bytes 4866048 | tf_op jit(solution)/shard_map/all_gather | solution.py:127
  103.7 524.1 %all-gather.27.cloned.1.call-start = ((), (), s32[]{:S(2)}) async-start(), calls=%async_computation.16 | async-start | bytes 3538944 | tf_op jit(solution)/shard_map/all_gather | solution.py:173
  103.9 74.8 %copy-start.189 = (bf16[768]{0:T(1024)(128)(2,1)S(1)}, bf16[768]{0:T(1024)(128)(2,1)}, u32[]{:S(2)}) copy-start(bf16[768]{0:T(1024)(128)(2,1)} %get-tuple-element.670) | copy-start | bytes 4612
  105.0 583.9 %all-gather.25.cloned.1.call-start = ((), (), s32[]{:S(2)}) async-start(), calls=%async_computation.14 | async-start | bytes 3538944 | tf_op jit(solution)/shard_map/all_gather | solution.py:173
  105.1 100.1 %copy-start.85 = (bf16[96,768]{1,0:T(8,128)(2,1)S(1)}, bf16[96,768]{1,0:T(8,128)(2,1)}, u32[]{:S(2)}) copy-start(bf16[96,768]{1,0:T(8,128)(2,1)} %get-tuple-element.685) | copy-start | bytes 442372
  105.1 12.7 collective-permute-start.14
  107.4 98.6 %copy-start.86 = (bf16[96,768]{1,0:T(8,128)(2,1)S(1)}, bf16[96,768]{1,0:T(8,128)(2,1)}, u32[]{:S(2)}) copy-start(bf16[96,768]{1,0:T(8,128)(2,1)} %get-tuple-element.682) | copy-start | bytes 442372
  107.4 23.7 %collective-permute-start.15 = (bf16[1,96,12,64]{1,3,2,0:T(8,128)(2,1)S(1)}, bf16[1,96,12,64]{1,3,2,0:T(8,128)(2,1)S(1)}, u32[]{:S(2)}, u32[]{:S(2)}) collective-permute-start(bf16[1,96,12,64]{1,3,2,0:T(8,128)(2,1)S(1)} %bitcast.715), channel_id=1, source_target_pairs={{0,7},{1,0},{2,1},{3,2},{4,3},{5,4},{6,5},{7,6},{8,15},{9,8},{10,9... | collective-permute-start | bytes 442376 | tf_op jit(solution)/shard_map/ppermute | solution.py:28
  110.6 26.4 %collective-permute-start.7 = (bf16[1,96,12,64]{1,3,2,0:T(8,128)(2,1)S(1)}, bf16[1,96,12,64]{1,3,2,0:T(8,128)(2,1)S(1)}, u32[]{:S(2)}, u32[]{:S(2)}) collective-permute-start(bf16[1,96,12,64]{1,3,2,0:T(8,128)(2,1)S(1)} %bitcast.718), channel_id=1, source_target_pairs={{0,1},{1,2},{2,3},{3,4},{4,5},{5,6},{6,7},{7,0},{8,9},{9,10},{10,1... | collective-permute-start | bytes 442376 | tf_op jit(solution)/shard_map/ppermute | solution.py:23
  110.6 33.9 %collective-permute-start.8 = (bf16[1,96,12,64]{1,3,2,0:T(8,128)(2,1)S(1)}, bf16[1,96,12,64]{1,3,2,0:T(8,128)(2,1)S(1)}, u32[]{:S(2)}, u32[]{:S(2)}) collective-permute-start(bf16[1,96,12,64]{1,3,2,0:T(8,128)(2,1)S(1)} %bitcast.719), channel_id=1, source_target_pairs={{0,7},{1,0},{2,1},{3,2},{4,3},{5,4},{6,5},{7,6},{8,15},{9,8},{10,9... | collective-permute-start | bytes 442376 | tf_op jit(solution)/shard_map/ppermute | solution.py:28
  115.5 32.5 %collective-permute-start = (bf16[1,96,12,64]{1,3,2,0:T(8,128)(2,1)S(1)}, bf16[1,96,12,64]{1,3,2,0:T(8,128)(2,1)S(1)}, u32[]{:S(2)}, u32[]{:S(2)}) collective-permute-start(bf16[1,96,12,64]{1,3,2,0:T(8,128)(2,1)S(1)} %bitcast.721), channel_id=1, source_target_pairs={{0,1},{1,2},{2,3},{3,4},{4,5},{5,6},{6,7},{7,0},{8,9},{9,10},{10,1... | collective-permute-start | bytes 442376 | tf_op jit(solution)/shard_map/ppermute | solution.py:23
  117.8 39.3 %collective-permute-start.1 = (bf16[1,96,12,64]{1,3,2,0:T(8,128)(2,1)S(1)}, bf16[1,96,12,64]{1,3,2,0:T(8,128)(2,1)S(1)}, u32[]{:S(2)}, u32[]{:S(2)}) collective-permute-start(bf16[1,96,12,64]{1,3,2,0:T(8,128)(2,1)S(1)} %bitcast.722), channel_id=1, source_target_pairs={{0,7},{1,0},{2,1},{3,2},{4,3},{5,4},{6,5},{7,6},{8,15},{9,8},{10,9... | collective-permute-start | bytes 442376 | tf_op jit(solution)/shard_map/ppermute | solution.py:28
  131.1 75.9 %copy-start.92 = (bf16[1,96,12,64]{1,3,2,0:T(8,128)(2,1)}, bf16[1,96,12,64]{1,3,2,0:T(8,128)(2,1)S(1)}, u32[]{:S(2)}) copy-start(bf16[1,96,12,64]{1,3,2,0:T(8,128)(2,1)S(1)} %collective-permute-done.15) | copy-start | bytes 442372
  131.1 29.5 %collective-permute-start.16 = (bf16[1,96,12,64]{1,3,2,0:T(8,128)(2,1)S(1)}, bf16[1,96,12,64]{1,3,2,0:T(8,128)(2,1)S(1)}, u32[]{:S(2)}, u32[]{:S(2)}) collective-permute-start(bf16[1,96,12,64]{1,3,2,0:T(8,128)(2,1)S(1)} %collective-permute-done.14), channel_id=1, source_target_pairs={{0,1},{1,2},{2,3},{3,4},{4,5},{5,6},{6,7},{7,0},{8,9},{9,10},{10,1... | collective-permute-start | bytes 442376 | tf_op jit(solution)/shard_map/ppermute | solution.py:23
  137.0 69.9 %copy-start.96 = (bf16[1,96,12,64]{1,3,2,0:T(8,128)(2,1)}, bf16[1,96,12,64]{1,3,2,0:T(8,128)(2,1)S(1)}, u32[]{:S(2)}) copy-start(bf16[1,96,12,64]{1,3,2,0:T(8,128)(2,1)S(1)} %collective-permute-done.7) | copy-start | bytes 442372
  137.1 32.7 %collective-permute-start.17 = (bf16[1,96,12,64]{1,3,2,0:T(8,128)(2,1)S(1)}, bf16[1,96,12,64]{1,3,2,0:T(8,128)(2,1)S(1)}, u32[]{:S(2)}, u32[]{:S(2)}) collective-permute-start(bf16[1,96,12,64]{1,3,2,0:T(8,128)(2,1)S(1)} %collective-permute-done.15), channel_id=1, source_target_pairs={{0,7},{1,0},{2,1},{3,2},{4,3},{5,4},{6,5},{7,6},{8,15},{9,8},{10,9... | collective-permute-start | bytes 442376 | tf_op jit(solution)/shard_map/ppermute | solution.py:28
  144.5 62.5 %copy-start.94 = (bf16[1,96,12,64]{1,3,2,0:T(8,128)(2,1)}, bf16[1,96,12,64]{1,3,2,0:T(8,128)(2,1)S(1)}, u32[]{:S(2)}) copy-start(bf16[1,96,12,64]{1,3,2,0:T(8,128)(2,1)S(1)} %collective-permute-done.8) | copy-start | bytes 442372
  144.5 26.4 %collective-permute-start.9 = (bf16[1,96,12,64]{1,3,2,0:T(8,128)(2,1)S(1)}, bf16[1,96,12,64]{1,3,2,0:T(8,128)(2,1)S(1)}, u32[]{:S(2)}, u32[]{:S(2)}) collective-permute-start(bf16[1,96,12,64]{1,3,2,0:T(8,128)(2,1)S(1)} %collective-permute-done.7), channel_id=1, source_target_pairs={{0,1},{1,2},{2,3},{3,4},{4,5},{5,6},{6,7},{7,0},{8,9},{9,10},{10,1... | collective-permute-start | bytes 442376 | tf_op jit(solution)/shard_map/ppermute | solution.py:23
  148.0 59.0 %copy-start.97 = (bf16[1,96,12,64]{1,3,2,0:T(8,128)(2,1)}, bf16[1,96,12,64]{1,3,2,0:T(8,128)(2,1)S(1)}, u32[]{:S(2)}) copy-start(bf16[1,96,12,64]{1,3,2,0:T(8,128)(2,1)S(1)} %collective-permute-done) | copy-start | bytes 442372
  148.0 28.2 %collective-permute-start.10 = (bf16[1,96,12,64]{1,3,2,0:T(8,128)(2,1)S(1)}, bf16[1,96,12,64]{1,3,2,0:T(8,128)(2,1)}, u32[]{:S(2)}, u32[]{:S(2)}) collective-permute-start(bf16[1,96,12,64]{1,3,2,0:T(8,128)(2,1)S(1)} %collective-permute-done.8), channel_id=1, source_target_pairs={{0,7},{1,0},{2,1},{3,2},{4,3},{5,4},{6,5},{7,6},{8,15},{9,8},{10,9... | collective-permute-start | bytes 442376 | tf_op jit(solution)/shard_map/ppermute | solution.py:28
  157.1 49.6 %copy-start.99 = (bf16[1,96,12,64]{1,3,2,0:T(8,128)(2,1)}, bf16[1,96,12,64]{1,3,2,0:T(8,128)(2,1)S(1)}, u32[]{:S(2)}) copy-start(bf16[1,96,12,64]{1,3,2,0:T(8,128)(2,1)S(1)} %collective-permute-done.1) | copy-start | bytes 442372
  157.1 19.1 %collective-permute-start.2 = (bf16[1,96,12,64]{1,3,2,0:T(8,128)(2,1)S(1)}, bf16[1,96,12,64]{1,3,2,0:T(8,128)(2,1)S(1)}, u32[]{:S(2)}, u32[]{:S(2)}) collective-permute-start(bf16[1,96,12,64]{1,3,2,0:T(8,128)(2,1)S(1)} %collective-permute-done), channel_id=1, source_target_pairs={{0,1},{1,2},{2,3},{3,4},{4,5},{5,6},{6,7},{7,0},{8,9},{9,10},{10,1... | collective-permute-start | bytes 442376 | tf_op jit(solution)/shard_map/ppermute | solution.py:23
  160.6 46.4 %copy-start.101 = (bf16[1,96,12,64]{1,3,2,0:T(8,128)(2,1)}, bf16[1,96,12,64]{1,3,2,0:T(8,128)(2,1)S(1)}, u32[]{:S(2)}) copy-start(bf16[1,96,12,64]{1,3,2,0:T(8,128)(2,1)S(1)} %collective-permute-done.16) | copy-start | bytes 442372
  160.6 22.8 %collective-permute-start.3 = (bf16[1,96,12,64]{1,3,2,0:T(8,128)(2,1)S(1)}, bf16[1,96,12,64]{1,3,2,0:T(8,128)(2,1)}, u32[]{:S(2)}, u32[]{:S(2)}) collective-permute-start(bf16[1,96,12,64]{1,3,2,0:T(8,128)(2,1)S(1)} %collective-permute-done.1), channel_id=1, source_target_pairs={{0,7},{1,0},{2,1},{3,2},{4,3},{5,4},{6,5},{7,6},{8,15},{9,8},{10,9... | collective-permute-start | bytes 442376 | tf_op jit(solution)/shard_map/ppermute | solution.py:28
  169.8 13.7 collective-permute-start.18
  170.9 21.2 %collective-permute-start.19 = (bf16[1,96,12,64]{1,3,2,0:T(8,128)(2,1)S(1)}, bf16[1,96,12,64]{1,3,2,0:T(8,128)(2,1)}, u32[]{:S(2)}, u32[]{:S(2)}) collective-permute-start(bf16[1,96,12,64]{1,3,2,0:T(8,128)(2,1)S(1)} %collective-permute-done.17), channel_id=1, source_target_pairs={{0,7},{1,0},{2,1},{3,2},{4,3},{5,4},{6,5},{7,6},{8,15},{9,8},{10,9... | collective-permute-start | bytes 442376 | tf_op jit(solution)/shard_map/ppermute | solution.py:28
  176.2 17.8 %collective-permute-start.11 = (bf16[1,96,12,64]{1,3,2,0:T(8,128)(2,1)S(1)}, bf16[1,96,12,64]{1,3,2,0:T(8,128)(2,1)}, u32[]{:S(2)}, u32[]{:S(2)}) collective-permute-start(bf16[1,96,12,64]{1,3,2,0:T(8,128)(2,1)S(1)} %collective-permute-done.9), channel_id=1, source_target_pairs={{0,1},{1,2},{2,3},{3,4},{4,5},{5,6},{6,7},{7,0},{8,9},{9,10},{10,1... | collective-permute-start | bytes 442376 | tf_op jit(solution)/shard_map/ppermute | solution.py:23
  176.2 24.1 %collective-permute-start.4 = (bf16[1,96,12,64]{1,3,2,0:T(8,128)(2,1)S(1)}, bf16[1,96,12,64]{1,3,2,0:T(8,128)(2,1)}, u32[]{:S(2)}, u32[]{:S(2)}) collective-permute-start(bf16[1,96,12,64]{1,3,2,0:T(8,128)(2,1)S(1)} %collective-permute-done.2), channel_id=1, source_target_pairs={{0,1},{1,2},{2,3},{3,4},{4,5},{5,6},{6,7},{7,0},{8,9},{9,10},{10,1... | collective-permute-start | bytes 442376 | tf_op jit(solution)/shard_map/ppermute | solution.py:23
  183.4 92.9 %collective-permute-start.12 = (bf16[1,96,12,64]{1,3,2,0:T(8,128)(2,1)}, bf16[1,96,12,64]{1,3,2,0:T(8,128)(2,1)}, u32[]{:S(2)}, u32[]{:S(2)}) collective-permute-start(bf16[1,96,12,64]{1,3,2,0:T(8,128)(2,1)} %collective-permute-done.10), channel_id=1, source_target_pairs={{0,7},{1,0},{2,1},{3,2},{4,3},{5,4},{6,5},{7,6},{8,15},{9,8},{10,9... | collective-permute-start | bytes 442376 | tf_op jit(solution)/shard_map/ppermute | solution.py:28
  183.5 110.5 %collective-permute-start.5 = (bf16[1,96,12,64]{1,3,2,0:T(8,128)(2,1)}, bf16[1,96,12,64]{1,3,2,0:T(8,128)(2,1)}, u32[]{:S(2)}, u32[]{:S(2)}) collective-permute-start(bf16[1,96,12,64]{1,3,2,0:T(8,128)(2,1)} %collective-permute-done.3), channel_id=1, source_target_pairs={{0,7},{1,0},{2,1},{3,2},{4,3},{5,4},{6,5},{7,6},{8,15},{9,8},{10,9... | collective-permute-start | bytes 442376 | tf_op jit(solution)/shard_map/ppermute | solution.py:28
  192.1 106.1 %collective-permute-start.20 = (bf16[1,96,12,64]{1,3,2,0:T(8,128)(2,1)}, bf16[1,96,12,64]{1,3,2,0:T(8,128)(2,1)}, u32[]{:S(2)}, u32[]{:S(2)}) collective-permute-start(bf16[1,96,12,64]{1,3,2,0:T(8,128)(2,1)} %collective-permute-done.18), channel_id=1, source_target_pairs={{0,1},{1,2},{2,3},{3,4},{4,5},{5,6},{6,7},{7,0},{8,9},{9,10},{10,1... | collective-permute-start | bytes 442376 | tf_op jit(solution)/shard_map/ppermute | solution.py:23
  194.0 106.8 %collective-permute-start.13 = (bf16[1,96,12,64]{1,3,2,0:T(8,128)(2,1)}, bf16[1,96,12,64]{1,3,2,0:T(8,128)(2,1)}, u32[]{:S(2)}, u32[]{:S(2)}) collective-permute-start(bf16[1,96,12,64]{1,3,2,0:T(8,128)(2,1)} %collective-permute-done.11), channel_id=1, source_target_pairs={{0,1},{1,2},{2,3},{3,4},{4,5},{5,6},{6,7},{7,0},{8,9},{9,10},{10,1... | collective-permute-start | bytes 442376 | tf_op jit(solution)/shard_map/ppermute | solution.py:23
  200.4 104.1 %collective-permute-start.6 = (bf16[1,96,12,64]{1,3,2,0:T(8,128)(2,1)}, bf16[1,96,12,64]{1,3,2,0:T(8,128)(2,1)}, u32[]{:S(2)}, u32[]{:S(2)}) collective-permute-start(bf16[1,96,12,64]{1,3,2,0:T(8,128)(2,1)} %collective-permute-done.4), channel_id=1, source_target_pairs={{0,1},{1,2},{2,3},{3,4},{4,5},{5,6},{6,7},{7,0},{8,9},{9,10},{10,1... | collective-permute-start | bytes 442376 | tf_op jit(solution)/shard_map/ppermute | solution.py:23
  204.1 121.9 %copy-start.81 = (pred[96,768]{1,0:T(8,128)(4,1)}, pred[96,768]{1,0:T(8,128)(4,1)S(1)}, u32[]{:S(2)}) copy-start(pred[96,768]{1,0:T(8,128)(4,1)S(1)} %get-tuple-element.730) | copy-start | bytes 221188
  215.3 571.2 %reduce-scatter.12.cloned.1.call-start = ((), (), s32[]{:S(2)}) async-start(), calls=%async_computation.19 | async-start | bytes 5308416 | tf_op jit(solution)/shard_map/reduce_scatter | solution.py:198
  320.0 262.2 %copy-start.6 = (f32[96,767]{0,1:T(8,128)}, f32[96,767]{0,1:T(8,128)S(1)}, u32[]{:S(2)}) copy-start(f32[96,767]{0,1:T(8,128)S(1)} %get-tuple-element.735) | copy-start | bytes 883588
  333.0 46.5 %copy-start.163 = (f32[96]{0:T(128)}, f32[96]{0:T(128)S(1)}, u32[]{:S(2)}) copy-start(f32[96]{0:T(128)S(1)} %get-tuple-element.582) | copy-start | bytes 1156
  333.0 46.5 %copy-start.165 = (f32[96]{0:T(128)}, f32[96]{0:T(128)S(1)}, u32[]{:S(2)}) copy-start(f32[96]{0:T(128)S(1)} %get-tuple-element.583) | copy-start | bytes 1156
  333.0 246.1 %copy-start.8 = (f32[96,767]{0,1:T(8,128)}, f32[96,767]{0,1:T(8,128)S(1)}, u32[]{:S(2)}) copy-start(f32[96,767]{0,1:T(8,128)S(1)} %get-tuple-element.740) | copy-start | bytes 883588
  333.0 239.2 %copy-start.145 = (f32[96,1]{0,1:T(1,128)}, f32[96,1]{0,1:T(1,128)S(1)}, u32[]{:S(2)}) copy-start(f32[96,1]{0,1:T(1,128)S(1)} %bitcast_negate_fusion.2) | copy-start | bytes 1156
  333.0 246.1 %copy-start.127 = (f32[96]{0:T(128)}, f32[96]{0:T(128)S(1)}, u32[]{:S(2)}) copy-start(f32[96]{0:T(128)S(1)} %fusion.267) | copy-start | bytes 1156
  333.1 46.4 %copy-start.80 = (pred[96,768]{1,0:T(8,128)(4,1)S(1)}, pred[96,768]{1,0:T(8,128)(4,1)}, u32[]{:S(2)}) copy-start(pred[96,768]{1,0:T(8,128)(4,1)} %get-tuple-element.728) | copy-start | bytes 221188
  385.0 55.3 %copy-start.64 = (bf16[1,96,12,64]{1,3,2,0:T(8,128)(2,1)}, bf16[1,96,12,64]{1,3,2,0:T(8,128)(2,1)S(1)}, u32[]{:S(2)}) copy-start(bf16[1,96,12,64]{1,3,2,0:T(8,128)(2,1)S(1)} %get-tuple-element.743) | copy-start | bytes 442372
  385.6 54.7 %copy-start.167 = (f32[96]{0:T(128)}, f32[96]{0:T(128)S(1)}, u32[]{:S(2)}) copy-start(f32[96]{0:T(128)S(1)} %get-tuple-element.580) | copy-start | bytes 1156
  385.6 54.7 %copy-start.169 = (f32[96]{0:T(128)}, f32[96]{0:T(128)S(1)}, u32[]{:S(2)}) copy-start(f32[96]{0:T(128)S(1)} %get-tuple-element.581) | copy-start | bytes 1156
  385.6 193.6 %copy-start.11 = (f32[96,767]{0,1:T(8,128)}, f32[96,767]{0,1:T(8,128)S(1)}, u32[]{:S(2)}) copy-start(f32[96,767]{0,1:T(8,128)S(1)} %get-tuple-element.745) | copy-start | bytes 883588
  385.6 190.8 %copy-start.148 = (f32[96,1]{0,1:T(1,128)}, f32[96,1]{0,1:T(1,128)S(1)}, u32[]{:S(2)}) copy-start(f32[96,1]{0,1:T(1,128)S(1)} %bitcast_negate_fusion.4) | copy-start | bytes 1156
  385.6 193.5 %copy-start.129 = (f32[96]{0:T(128)}, f32[96]{0:T(128)S(1)}, u32[]{:S(2)}) copy-start(f32[96]{0:T(128)S(1)} %fusion.265) | copy-start | bytes 1156
  385.6 115.3 %copy-start.139 = (f32[96,1]{0,1:T(1,128)S(1)}, f32[96,1]{0,1:T(1,128)}, u32[]{:S(2)}) copy-start(f32[96,1]{0,1:T(1,128)} %bitcast_negate_fusion) | copy-start | bytes 1156
  385.6 115.2 %copy-start.142 = (f32[96]{0:T(128)S(1)}, f32[96]{0:T(128)}, u32[]{:S(2)}) copy-start(f32[96]{0:T(128)} %fusion.269) | copy-start | bytes 1156
  617.9 267.2 %reduce-scatter.10.cloned.1.call-start = ((), (), s32[]{:S(2)}) async-start(), calls=%async_computation.17 | async-start | bytes 5308416 | tf_op jit(solution)/shard_map/reduce_scatter | solution.py:198
  669.8 313.9 %reduce-scatter.8.cloned.1.call-start = ((), (), s32[]{:S(2)}) async-start(), calls=%async_computation.15 | async-start | bytes 5308416 | tf_op jit(solution)/shard_map/reduce_scatter | solution.py:198
  724.1 364.3 %reduce-scatter.16.cloned.1.call-start = ((), (), s32[]{:S(2)}) async-start(), calls=%async_computation.21 | async-start | bytes 2433024 | tf_op jit(solution)/shard_map/reduce_scatter | solution.py:322
  728.6 501.8 %reduce-scatter.20.cloned.1.call-start = ((), (), s32[]{:S(2)}) async-start(), calls=%async_computation.23 | async-start | bytes 9732096 | tf_op jit(solution)/shard_map/reduce_scatter | solution.py:324
  738.3 633.0 %reduce-scatter.18.cloned.1.call-start = ((), (), s32[]{:S(2)}) async-start(), calls=%async_computation.22 | async-start | bytes 9732096 | tf_op jit(solution)/shard_map/reduce_scatter | solution.py:323
  748.4 748.0 %reduce-scatter.14.cloned.1.call-start = ((), (), s32[]{:S(2)}) async-start(), calls=%async_computation.20 | async-start | bytes 7299072 | tf_op jit(solution)/shard_map/reduce_scatter | solution.py:321
  (194 other events, 922.8 us)
Sparse Core Ops, SparseCore 0:
  10.9 62.9 all-gather.10
  81.8 102.3 all-gather.22
  187.2 63.9 all-gather.14
  253.8 59.4 all-gather.20
  315.4 59.1 all-gather.12
  376.6 59.0 all-gather.28
  438.6 62.2 all-gather.16
  503.8 62.4 all-gather.18
  568.5 59.2 all-gather.26
  629.8 59.0 all-gather.24
  692.6 93.8 reduce-scatter.11
  790.0 94.9 reduce-scatter.9
  888.7 95.0 reduce-scatter.7
  989.4 98.9 reduce-scatter.15
  1095.7 134.5 reduce-scatter.19
  1236.7 134.4 reduce-scatter.17
  1378.3 118.0 reduce-scatter.13
